TPU v7x, 32 devices: a whole 2x2x4 slice. The times are simulated.
32 devices in a mesh: parts: 1, axial: 8 (over y, x, core), radial: 4 (over z).
Axes of the slice: x: 2, y: 2, z: 4, core: 2. Of those that a mesh axis runs over, the one named last changes fastest.
Arguments:
- inputs: bfloat16 [64, 64, 8192], P(None, 'radial', ('parts', 'axial')), may hold values from -6 to 6
- saved_pre: bfloat16 [64, 64, 8192], P(None, 'radial', ('parts', 'axial')), may hold values from -6 to 6
- cotangent: bfloat16 [64, 64, 8192], P(None, 'radial', ('parts', 'axial')), may hold values from -24 to 24
- pointwise_weight: bfloat16 [64, 64], replicated, may hold values from -0.75 to 0.75
- spectral_weight: bfloat16 [32, 256, 64, 128], P('radial', 'axial'), may hold values from -3 to 3
Outputs:
- input_grad: bfloat16 [64, 64, 8192], P(None, 'radial', ('parts', 'axial'))
- spectral_grad: float32 [32, 256, 64, 128], P('radial', ('parts', 'axial'))
- weight_grad: float32 [64, 64], P('parts')
All inputs are finite; a program needn't handle non-finite values.
Results may differ from a plain program's by a relative error of at most 0.0053.
Values may be sent and summed in bfloat16 or wider, within the bound.
A program may use at most 128 MiB of HBM per device.

v0:
```python
import math

import jax
import jax.numpy as jnp
from jax import lax
from jax.sharding import PartitionSpec as P

KA = 256
KR = 32


def axial_table(first, count, modes, total):
    points = first + jnp.arange(count, dtype=jnp.int32)
    orders = jnp.arange(modes, dtype=jnp.int32)
    phase = (points[:, None] * orders[None, :] % total).astype(jnp.float32) * (
        2.0 * math.pi / total
    )
    return (
        jnp.stack([jnp.cos(phase), -jnp.sin(phase)], axis=2)
        .reshape(count, 2 * modes)
        .astype(jnp.bfloat16)
    )


def radial_table(count, rows_first, rows_count, kept, total):
    orders = jnp.arange(count, dtype=jnp.int32)
    freqs = orders + jnp.where(orders >= kept // 2, total - kept, 0).astype(jnp.int32)
    rows = rows_first + jnp.arange(rows_count, dtype=jnp.int32)
    phase = (freqs[:, None] * rows[None, :] % total).astype(jnp.float32) * (2.0 * math.pi / total)
    return (jnp.cos(phase), jnp.sin(phase))


def gelu_slope(pre):
    value = pre.astype(jnp.float32)
    return 0.5 * (1.0 + jax.scipy.special.erf(value / math.sqrt(2.0))) + value * jnp.exp(
        -0.5 * value * value
    ) / math.sqrt(2.0 * math.pi)


def to_modes(axial_part, cos_r, sin_r, own_ax, channels, rad_rows):
    split = axial_part.reshape(own_ax, 2, channels, rad_rows)
    real_in = split[:, 0]
    imag_in = split[:, 1]
    high = lax.Precision.HIGHEST
    real_out = jnp.einsum("qr,kcr->qkc", cos_r, real_in, precision=high) + jnp.einsum(
        "qr,kcr->qkc", sin_r, imag_in, precision=high
    )
    imag_out = jnp.einsum("qr,kcr->qkc", cos_r, imag_in, precision=high) - jnp.einsum(
        "qr,kcr->qkc", sin_r, real_in, precision=high
    )
    return (real_out, imag_out)


def body(inputs, saved_pre, cotangent, pointwise_weight, spectral_weight):
    high = lax.Precision.HIGHEST
    channels, rad_rows, ax_cols = inputs.shape
    n_axial = lax.axis_size("axial")
    n_radial = lax.axis_size("radial")
    ax_index = lax.axis_index("axial")
    rad_index = lax.axis_index("radial")
    axial_total = ax_cols * n_axial
    radial_total = rad_rows * n_radial
    own_ax = KA // n_axial
    grad_pre = (cotangent.astype(jnp.float32) * gelu_slope(saved_pre)).astype(jnp.bfloat16)
    table = axial_table(ax_index * ax_cols, ax_cols, KA, axial_total)
    columns = table
    part_in = jnp.einsum("cra,aj->jcr", inputs, columns, preferred_element_type=jnp.float32)
    part_grad = jnp.einsum("cra,aj->jcr", grad_pre, columns, preferred_element_type=jnp.float32)
    summed = lax.psum_scatter(
        jnp.concatenate(
            [
                part_in.reshape(2 * own_ax * lax.axis_size("axial"), -1),
                part_grad.reshape(2 * own_ax * lax.axis_size("axial"), -1),
            ],
            axis=1,
        ),
        "axial",
        scatter_dimension=0,
        tiled=True,
    )
    half = channels * rad_rows
    spec_in = summed[:, :half].reshape(2 * own_ax, channels, rad_rows)
    spec_grad = summed[:, half:].reshape(2 * own_ax, channels, rad_rows)
    cos_r, sin_r = radial_table(KR, rad_index * rad_rows, rad_rows, KR, radial_total)
    x_real, x_imag = to_modes(spec_in, cos_r, sin_r, own_ax, channels, rad_rows)
    g_real, g_imag = to_modes(spec_grad, cos_r, sin_r, own_ax, channels, rad_rows)
    stacked = jnp.stack([x_real, x_imag, g_real, g_imag], axis=1)
    owned = lax.psum_scatter(stacked, "radial", scatter_dimension=0, tiled=True)
    orders = ax_index * own_ax + jnp.arange(own_ax, dtype=jnp.int32)
    scales = jnp.where(orders == 0, 1.0, 2.0).astype(jnp.float32) / (radial_total * axial_total)
    x_real = owned[:, 0]
    x_imag = owned[:, 1]
    dy_real = owned[:, 2] * scales[None, :, None]
    dy_imag = owned[:, 3] * scales[None, :, None]
    grad_real = (
        x_real[..., :, None] * dy_real[..., None, :] + x_imag[..., :, None] * dy_imag[..., None, :]
    )
    grad_imag = (
        x_real[..., :, None] * dy_imag[..., None, :] - x_imag[..., :, None] * dy_real[..., None, :]
    )
    spectral_grad = jnp.concatenate([grad_real, grad_imag], axis=3)
    w_real = spectral_weight[..., :channels].astype(jnp.float32)
    w_imag = spectral_weight[..., channels:].astype(jnp.float32)
    dx_real = jnp.einsum("qkio,qko->qki", w_real, dy_real, precision=high) + jnp.einsum(
        "qkio,qko->qki", w_imag, dy_imag, precision=high
    )
    dx_imag = jnp.einsum("qkio,qko->qki", w_real, dy_imag, precision=high) - jnp.einsum(
        "qkio,qko->qki", w_imag, dy_real, precision=high
    )
    mode_grad = jnp.stack([dx_real, dx_imag], axis=1)
    row_first = rad_index * rad_rows
    piece = lax.all_gather(mode_grad, "radial", axis=0, tiled=True)
    cos_q, sin_q = radial_table(piece.shape[0], row_first, rad_rows, KR, radial_total)
    piece_real = piece[:, 0]
    piece_imag = piece[:, 1]
    out_real = jnp.einsum("qr,qkc->kcr", cos_q, piece_real, precision=high) - jnp.einsum(
        "qr,qkc->kcr", sin_q, piece_imag, precision=high
    )
    out_imag = jnp.einsum("qr,qkc->kcr", sin_q, piece_real, precision=high) + jnp.einsum(
        "qr,qkc->kcr", cos_q, piece_imag, precision=high
    )
    back = jnp.stack([out_real, out_imag], axis=1)
    lines_back = back.astype(jnp.bfloat16).reshape(2 * own_ax, channels * rad_rows)
    columns = table
    spectral_part = jnp.einsum(
        "jm,aj->ma",
        lax.all_gather(lines_back, "axial", axis=0, tiled=True),
        columns,
        preferred_element_type=jnp.float32,
    )
    flat_grad = grad_pre.reshape(channels, rad_rows * ax_cols)
    flat_in = inputs.reshape(channels, rad_rows * ax_cols)
    point_part = jnp.dot(pointwise_weight, flat_grad, preferred_element_type=jnp.float32)
    input_grad = (
        (point_part + spectral_part.reshape(channels, rad_rows * ax_cols))
        .astype(jnp.bfloat16)
        .reshape(channels, rad_rows, ax_cols)
    )
    local_weight = lax.dot_general(
        flat_in, flat_grad, (((1,), (1,)), ((), ())), preferred_element_type=jnp.float32
    )
    weight_grad = lax.psum(local_weight, ("axial", "radial")) / math.sqrt(
        radial_total * axial_total
    )
    return (input_grad, spectral_grad, weight_grad)


def solution(mesh):
    placed = (
        P(None, "radial", ("parts", "axial")),
        P(None, "radial", ("parts", "axial")),
        P(None, "radial", ("parts", "axial")),
        P(),
        P("radial", "axial", None, None),
    )
    return jax.shard_map(
        body,
        mesh=mesh,
        in_specs=placed,
        out_specs=(
            P(None, "radial", ("parts", "axial")),
            P("radial", ("parts", "axial"), None, None),
            P("parts", None),
        ),
        check_vma=False,
    )
```

profile of v0, /device:TPU:0, one launch (start us, length us, event | category | flops | bytes accessed | tf_op | source)
XLA Modules:
  0.0 311.8 jit_solution(6213764440670143054)
XLA Ops:
  7.2 5.0 %fusion.44 = (bf16[1024,256,1]{1,0,2:T(8,128)(2,1)S(1)}, bf16[1024,256,1]{1,0,2:T(8,128)(2,1)S(1)}) fusion(s32[1024]{0:T(1024)S(1)} %iota_add_fusion), kind=kLoop, calls=%fused_computation.67 | loop fusion | flops 4456448 | bytes 1052672 | tf_op jit(solution)/shard_map/cos | solution.py:19
  12.4 2.1 copy.31
  16.0 3.9 %fusion.9 = bf16[64,16,1024]{2,1,0:T(8,128)(2,1)S(1)} fusion(bf16[64,16,1024]{2,1,0:T(8,128)(2,1)} %param.6, bf16[64,16,1024]{2,1,0:T(8,128)(2,1)} %param.7), kind=kLoop, calls=%fused_computation.18 | loop fusion | flops 12582912 | bytes 6291456 | tf_op jit(solution)/shard_map/convert_element_type | solution.py:64
  22.5 2.5 pad_maximum_fusion.1
  25.4 53.9 %reduce-scatter.3.cloned.1.call-done = f32[64,2048]{1,0:T(8,128)} async-done(((f32[512,2048]{1,0:T(8,128)}), f32[64,2048]{1,0:T(8,128)}) %reduce-scatter.3.cloned.1.call-update) | async-done | bytes 524304 | tf_op jit(solution)/shard_map/reduce_scatter | solution.py:69
  80.3 2.0 reshape_reshape.6
  82.4 4.3 %fusion.41 = f32[32,32,64]{2,0,1:T(8,128)S(1)} fusion(f32[32,2,64,16]{3,2,1,0:T(8,128)} %reshape_reshape.6, s32[16]{0:T(128)S(1)} %iota_add_fusion.1, s32[32]{0:T(128)S(1)} %fusion.84), kind=kOutput, calls=%fused_computation.62 | convolution fusion | flops 12590080 | bytes 1310912 | tf_op jit(solution)/shard_map/qr,kcr->qkc/dot_general | solution.py:48
  86.7 4.3 %fusion.40 = f32[32,32,64]{2,0,1:T(8,128)S(1)} fusion(f32[32,2,64,16]{3,2,1,0:T(8,128)} %reshape_reshape.6, s32[16]{0:T(128)S(1)} %iota_add_fusion.1, s32[32]{0:T(128)S(1)} %fusion.84), kind=kOutput, calls=%fused_computation.61 | convolution fusion | flops 12590080 | bytes 1310912 | tf_op jit(solution)/shard_map/qr,kcr->qkc/dot_general | solution.py:45
  91.0 2.0 reshape_reshape.7
  93.1 4.5 %fusion.43 = f32[32,32,64]{2,0,1:T(8,128)S(1)} fusion(f32[32,2,64,16]{3,2,1,0:T(8,128)} %reshape_reshape.7, s32[16]{0:T(128)S(1)} %iota_add_fusion.1, s32[32]{0:T(128)S(1)} %fusion.84), kind=kOutput, calls=%fused_computation.64 | convolution fusion | flops 12590080 | bytes 1310912 | tf_op jit(solution)/shard_map/qr,kcr->qkc/dot_general | solution.py:48
  97.6 4.3 %fusion.42 = f32[32,32,64]{2,0,1:T(8,128)S(1)} fusion(f32[32,2,64,16]{3,2,1,0:T(8,128)} %reshape_reshape.7, s32[16]{0:T(128)S(1)} %iota_add_fusion.1, s32[32]{0:T(128)S(1)} %fusion.84), kind=kOutput, calls=%fused_computation.63 | convolution fusion | flops 12590080 | bytes 1310912 | tf_op jit(solution)/shard_map/qr,kcr->qkc/dot_general | solution.py:45
  101.9 4.4 %fusion.23 = f32[32,1,32,64]{3,0,2,1:T(8,128)S(1)} fusion(f32[32,32,64]{2,0,1:T(8,128)S(1)} %fusion.41, f32[32,2,64,16]{3,2,1,0:T(8,128)} %reshape_reshape.6, s32[16]{0:T(128)S(1)} %iota_add_fusion.1, s32[32]{0:T(128)S(1)} %fusion.84), kind=kOutput, calls=%fused_computation.40 | convolution fusion | flops 12655616 | bytes 1573056 | tf_op jit(solution)/shard_map/qr,kcr->qkc/dot_general | solution.py:48
  106.3 3.2 %fusion.24 = f32[32,1,32,64]{3,0,2,1:T(8,128)S(1)} fusion(f32[32,32,64]{2,0,1:T(8,128)S(1)} %fusion.40, f32[32,2,64,16]{3,2,1,0:T(8,128)S(1)} %copy-done.2, s32[16]{0:T(128)S(1)} %iota_add_fusion.1, s32[32]{0:T(128)S(1)} %fusion.84), kind=kOutput, calls=%fused_computation.42 | convolution fusion | flops 12655616 | bytes 1836032 | tf_op jit(solution)/shard_map/qr,kcr->qkc/dot_general | solution.py:45
  109.5 3.6 %fusion.21 = f32[32,1,32,64]{3,0,2,1:T(8,128)S(1)} fusion(f32[32,32,64]{2,0,1:T(8,128)S(1)} %fusion.43, f32[32,2,64,16]{3,2,1,0:T(8,128)S(1)} %copy-done.3, s32[16]{0:T(128)S(1)} %iota_add_fusion.1, s32[32]{0:T(128)S(1)} %fusion.84), kind=kOutput, calls=%fused_computation.36 | convolution fusion | flops 12655616 | bytes 1836032 | tf_op jit(solution)/shard_map/qr,kcr->qkc/dot_general | solution.py:48
  113.1 3.1 %fusion.22 = f32[32,1,32,64]{3,0,2,1:T(8,128)S(1)} fusion(f32[32,32,64]{2,0,1:T(8,128)S(1)} %fusion.42, f32[32,2,64,16]{3,2,1,0:T(8,128)S(1)} %copy-done.3, s32[16]{0:T(128)S(1)} %iota_add_fusion.1, s32[32]{0:T(128)S(1)} %fusion.84), kind=kOutput, calls=%fused_computation.38 | convolution fusion | flops 12655616 | bytes 1836032 | tf_op jit(solution)/shard_map/qr,kcr->qkc/dot_general | solution.py:45
  116.2 1.6 pad_maximum_fusion.2
  117.9 44.0 %reduce-scatter.5.cloned.1.call-done = f32[8,4,32,64]{3,0,2,1:T(8,128)} async-done(((f32[32,4,32,64]{3,0,2,1:T(8,128)}), f32[8,4,32,64]{3,0,2,1:T(8,128)}) %reduce-scatter.5.cloned.1.call-update) | async-done | bytes 262160 | tf_op jit(solution)/shard_map/reduce_scatter | solution.py:88
  163.1 8.6 %fusion.10 = f32[8,32,1,64]{3,2,1,0:T(1,128)S(1)} fusion(bf16[8,32,64,128]{3,2,1,0:T(8,128)(2,1)} %param.9, f32[8,32,64,1]{2,0,1,3:T(8,128)S(1)} %bitcast.134), kind=kOutput, calls=%fused_computation.19 | convolution fusion | flops 12582912 | bytes 4325376 | tf_op jit(solution)/shard_map/qkio,qko->qki/dot_general | solution.py:107
  171.7 6.6 %fusion.16 = f32[8,32,1,64]{3,2,1,0:T(1,128)S(1)} fusion(bf16[8,32,64,128]{3,2,1,0:T(8,128)(2,1)S(1)} %copy-done.11, f32[8,32,64,1]{2,0,1,3:T(8,128)S(1)} %bitcast.135), kind=kOutput, calls=%fused_computation.25 | convolution fusion | flops 12582912 | bytes 4325376 | tf_op jit(solution)/shard_map/qkio,qko->qki/dot_general | solution.py:104
  178.3 6.6 %fusion.14 = f32[8,32,1,64]{3,2,1,0:T(1,128)S(1)} fusion(bf16[8,32,64,128]{3,2,1,0:T(8,128)(2,1)S(1)} %copy-done.11, f32[8,32,64,1]{2,0,1,3:T(8,128)S(1)} %bitcast.136), kind=kOutput, calls=%fused_computation.23 | convolution fusion | flops 12582912 | bytes 4325376 | tf_op jit(solution)/shard_map/qkio,qko->qki/dot_general | solution.py:107
  184.9 6.7 %fusion.12 = f32[8,32,1,64]{3,2,1,0:T(1,128)S(1)} fusion(bf16[8,32,64,128]{3,2,1,0:T(8,128)(2,1)S(1)} %copy-done.11, f32[8,32,64,1]{2,0,1,3:T(8,128)S(1)} %bitcast.137), kind=kOutput, calls=%fused_computation.21 | convolution fusion | flops 12582912 | bytes 4325376 | tf_op jit(solution)/shard_map/qkio,qko->qki/dot_general | solution.py:104
  191.9 21.4 %all_gather.6 = f32[32,2,32,64]{3,0,2,1:T(8,128)S(1)} all-gather(f32[8,2,32,64]{3,0,2,1:T(8,128)S(1)} %pad_maximum_fusion.3), channel_id=1, replica_groups=mesh['parts'=1,'axial'=8,'radial'=4] {'radial'}, dimensions={0}, use_global_device_ids=true | all-gather | bytes 655360 | tf_op jit(solution)/shard_map/all_gather | solution.py:112
  215.8 2.4 convert_element_type.61
  218.3 6.1 %fusion.29 = f32[64,64]{0,1:T(8,128)S(1)} fusion(bf16[64,16,1024]{2,1,0:T(8,128)(2,1)S(1)} %copy-done, bf16[64,16,1024]{2,1,0:T(8,128)(2,1)} %copy-done.4), kind=kOutput, calls=%fused_computation.49 | convolution fusion | flops 134217728 | bytes 4210688 | tf_op jit(solution)/shard_map/dot_general | solution.py:139
  224.4 39.2 %psum.7 = f32[64,64]{0,1:T(8,128)S(1)} all-reduce(f32[64,64]{0,1:T(8,128)S(1)} %fusion.29), channel_id=1, replica_groups=mesh['parts'=1,'axial'=8,'radial'=4] {'axial','radial'}, use_global_device_ids=true, to_apply=%region_2.3 | all-reduce | flops 4096 | bytes 32768 | tf_op jit(solution)/shard_map/psum | solution.py:142
  264.4 4.2 %copy.54 = bf16[8,8,16,1024]{3,1,2,0:T(8,128)(2,1)} copy(bf16[8,8,16,1024]{3,2,1,0:T(8,128)(2,1)} %bitcast.130) | data formatting | bytes 4194304
  268.7 8.5 %multiply_add_fusion = (f32[8,32,64,64]{3,2,1,0:T(8,128)}, f32[8,32,64,64]{3,2,1,0:T(8,128)}) fusion(f32[8,32,64]{2,1,0:T(8,128)S(1)} %copy.40, f32[8,32,64]{2,1,0:T(8,128)S(1)} %copy.39, f32[8,32,64]{2,1,0:T(8,128)S(1)} %copy.38, f32[8,32,64]{2,1,0:T(8,128)S(1)} %copy.37), kind=kLoop, calls=%fused_computation.5 | loop fusion | flops 6291456 | bytes 8650752 | tf_op jit(solution)/shard_map/add | solution.py:96
  277.2 12.2 %pad_maximum_fusion = f32[8,32,64,128]{3,2,1,0:T(8,128)} fusion(f32[8,32,64,64]{3,2,1,0:T(8,128)} %get-tuple-element.15, f32[8,32,64,64]{3,2,1,0:T(8,128)} %get-tuple-element.14), kind=kLoop, calls=%fused_computation.3 | loop fusion | flops 2097152 | bytes 16777216 | tf_op jit(solution)/shard_map/concatenate | solution.py:101
  289.4 4.5 %fusion.137 = f32[1024,1024]{1,0:T(8,128)} fusion(bf16[512,1024]{1,0:T(8,128)(2,1)} %all-gather.2.cloned.1.call-done, bf16[1024,512]{0,1:T(8,128)(2,1)S(1)} %copy-done.6), kind=kOutput, calls=%fused_computation.166 | convolution fusion | flops 1073741824 | bytes 6291456 | tf_op jit(solution)/shard_map/jm,aj->ma/dot_general | solution.py:125
  293.9 5.0 %reshape.173 = f32[64,16384]{1,0:T(8,128)} reshape(f32[1024,1024]{1,0:T(8,128)} %fusion.137) | data formatting | bytes 8388608 | tf_op jit(solution)/shard_map/reshape | solution.py:135
  298.9 3.7 %fusion.1 = bf16[64,16384]{1,0:T(8,128)(2,1)S(1)} fusion(f32[64,16384]{1,0:T(8,128)} %reshape.173, bf16[64,64]{1,0:T(8,128)(2,1)S(1)} %copy-done.10, bf16[64,16384]{1,0:T(8,128)(2,1)} %bitcast.131), kind=kOutput, calls=%fused_computation.2 | convolution fusion | flops 136314880 | bytes 8396800 | tf_op jit(solution)/shard_map/dot_general | solution.py:133
  302.5 2.5 copy.55
  (56 shorter events, 10.6 us)
Async XLA Ops:
  7.2 14.1 %copy-start = (bf16[64,16,1024]{2,1,0:T(8,128)(2,1)S(1)}, bf16[64,16,1024]{2,1,0:T(8,128)(2,1)}, u32[]{:S(2)}) copy-start(bf16[64,16,1024]{2,1,0:T(8,128)(2,1)} %param.5) | copy-start | bytes 6291460
  7.2 72.1 %reduce-scatter.3.cloned.1.call-start = ((), (), s32[]{:S(2)}) async-start(), calls=%async_computation.2 | async-start | bytes 4718592 | tf_op jit(solution)/shard_map/reduce_scatter | solution.py:69
  16.0 5.3 %copy-start.5 = (bf16[1024,512]{0,1:T(8,128)(2,1)}, bf16[1024,512]{0,1:T(8,128)(2,1)S(1)}, u32[]{:S(2)}) copy-start(bf16[1024,512]{0,1:T(8,128)(2,1)S(1)} %convert_element_type.60) | copy-start | bytes 3145732
  19.9 1.3 copy-start.4
  25.1 136.8 %reduce-scatter.5.cloned.1.call-start = ((), (), s32[]{:S(2)}) async-start(), calls=%async_computation.3 | async-start | bytes 2621440 | tf_op jit(solution)/shard_map/reduce_scatter | solution.py:88
  93.1 13.2 %copy-start.2 = (f32[32,2,64,16]{3,2,1,0:T(8,128)S(1)}, f32[32,2,64,16]{3,2,1,0:T(8,128)}, u32[]{:S(2)}) copy-start(f32[32,2,64,16]{3,2,1,0:T(8,128)} %reshape_reshape.6) | copy-start | bytes 786436
  93.1 16.4 %copy-start.3 = (f32[32,2,64,16]{3,2,1,0:T(8,128)S(1)}, f32[32,2,64,16]{3,2,1,0:T(8,128)}, u32[]{:S(2)}) copy-start(f32[32,2,64,16]{3,2,1,0:T(8,128)} %reshape_reshape.7) | copy-start | bytes 786436
  117.8 171.6 %all-gather.2.cloned.1.call-start = ((), (), s32[]{:S(2)}) async-start(), calls=%async_computation.4 | async-start | bytes 1179648 | tf_op jit(solution)/shard_map/all_gather | solution.py:127
  161.8 9.9 %copy-start.11 = (bf16[8,32,64,128]{3,2,1,0:T(8,128)(2,1)S(1)}, bf16[8,32,64,128]{3,2,1,0:T(8,128)(2,1)}, u32[]{:S(2)}) copy-start(bf16[8,32,64,128]{3,2,1,0:T(8,128)(2,1)} %param.9) | copy-start | bytes 12582916
  163.1 21.8 %copy-start.7 = (f32[8,32,64]{2,0,1:T(8,128)}, f32[8,32,64]{2,0,1:T(8,128)S(1)}, u32[]{:S(2)}) copy-start(f32[8,32,64]{2,0,1:T(8,128)S(1)} %get-tuple-element.12) | copy-start | bytes 196612
  218.3 50.3 %copy-start.8 = (f32[8,32,64]{2,0,1:T(8,128)S(1)}, f32[8,32,64]{2,0,1:T(8,128)}, u32[]{:S(2)}) copy-start(f32[8,32,64]{2,0,1:T(8,128)} %copy-done.7) | copy-start | bytes 196612
  218.3 50.3 %copy-start.9 = (f32[8,4,32,64]{3,0,2,1:T(8,128)S(1)}, f32[8,4,32,64]{3,0,2,1:T(8,128)}, u32[]{:S(2)}) copy-start(f32[8,4,32,64]{3,0,2,1:T(8,128)} %reduce-scatter.5.cloned.1.call-done) | copy-start | bytes 786436
  277.2 12.2 %copy-start.6 = (bf16[1024,512]{0,1:T(8,128)(2,1)S(1)}, bf16[1024,512]{0,1:T(8,128)(2,1)}, u32[]{:S(2)}) copy-start(bf16[1024,512]{0,1:T(8,128)(2,1)} %copy-done.5) | copy-start | bytes 3145732
  293.9 5.0 %copy-start.10 = (bf16[64,64]{1,0:T(8,128)(2,1)S(1)}, bf16[64,64]{1,0:T(8,128)(2,1)}, u32[]{:S(2)}) copy-start(bf16[64,64]{1,0:T(8,128)(2,1)} %param.8) | copy-start | bytes 24580
  298.9 6.2 %copy-start.1 = (bf16[64,16,1024]{2,1,0:T(8,128)(2,1)S(1)}, bf16[64,16,1024]{2,1,0:T(8,128)(2,1)}, u32[]{:S(2)}) copy-start(bf16[64,16,1024]{2,1,0:T(8,128)(2,1)} %param.5) | copy-start | bytes 6291460
Sparse Core Ops, SparseCore 0:
  25.2 53.9 reduce-scatter.2
  117.9 43.8 reduce-scatter.4
  218.4 23.6 all-gather.1
where the time goes:
time: 316 us; the launch traced here: 312 us
  waiting for transfers between devices  97.9 us (31%)
  matrix products  79 us (25%)
  blocking collectives  60.6 us (19%)
  other arithmetic  35.4 us (11%)
  local copies, waits for them, and re-layouts  24.2 us (8%)
  between operations  14.4 us (5%)
    reduce_scatter x1, waiting for transfers between devices, body(): lax.psum_scatter(jnp.concatenate([part_in.reshape(2 * own_ax * lax.axis_s...  53.9 us
    reduce_scatter x1, waiting for transfers between devices, body(): owned = lax.psum_scatter(stacked, 'radial', scatter_dimension=0, tiled=True)  44 us
    psum x1, blocking collectives, body(): lax.psum(local_weight, ('axial', 'radial'))  39.2 us
    all_gather x1, blocking collectives, body(): piece = lax.all_gather(mode_grad, 'radial', axis=0, tiled=True)  21.4 us
    concatenate x1, other arithmetic, body(): spectral_grad = jnp.concatenate([grad_real, grad_imag], axis=3)  12.2 us
    dot_general x2, matrix products, to_modes(): jnp.einsum('qr,kcr->qkc', cos_r, imag_in, precision=high)  8.81 us
    dot_general x2, matrix products, to_modes(): jnp.einsum('qr,kcr->qkc', cos_r, real_in, precision=high)  8.67 us
    dot_general x1, matrix products, body(): jnp.einsum('qkio,qko->qki', w_imag, dy_real, precision=high)  8.64 us
  transfers between devices with their start and end apart: 3, of which 2 were waited for; matrix products, arithmetic and copies ran while one was open for 10% of the time, Pallas kernels for 0%

commit v1 on v0

v1 whole, which is shorter than its diff:
```python
import functools
import math

import jax
import jax.numpy as jnp
import numpy as np
from jax import lax
from jax.experimental import pallas as pl
from jax.experimental.pallas import tpu as pltpu
from jax.sharding import PartitionSpec as P

KA = 256
KR = 32
LANES = 128
BF = jnp.bfloat16
F32 = jnp.float32
VMEM_LIMIT = 56 * 1024 * 1024


def axial_factors(n_axial, ax_cols):
    total = n_axial * ax_cols
    own = KA // n_axial
    col = np.arange(2 * KA)
    mode = (col // (2 * own)) * own + col % own
    turn = (col // own) % 2
    points = np.arange(LANES)
    low = (points[:, None] * mode[None, :] % total) * (2.0 * np.pi / total)
    starts = np.arange(total // LANES) * LANES
    high = (starts[:, None] * mode[None, :] % total) * (2.0 * np.pi / total)
    high = high + turn[None, :] * (np.pi / 2)
    as32 = lambda value: value.astype(np.float32)
    return as32(np.cos(low)), as32(np.sin(low)), as32(np.cos(high)), as32(np.sin(high))


def split16(value):
    high = value.astype(BF)
    return high, (value - high.astype(F32)).astype(BF)


def gelu_slope(value):
    return 0.5 * (1.0 + lax.erf(value * (1.0 / math.sqrt(2.0)))) + value * jnp.exp(
        -0.5 * value * value
    ) * (1.0 / math.sqrt(2.0 * math.pi))


def local_kernel(
    n_axial, x_ref, s_ref, c_ref, cl_ref, sl_ref, ch_ref, sh_ref, px_ref, pg_ref, grad_ref, table
):
    _, some, rad_rows, cols = x_ref.shape
    lines = some * rad_rows
    half = 2 * KA // n_axial
    pieces = cols // LANES

    @pl.when(pl.program_id(0) == 0)
    def _():
        first = lax.axis_index("axial") * pieces
        for u in range(pieces):
            at = pl.ds(first + u, 1)
            table[u * LANES : (u + 1) * LANES, :] = (
                ch_ref[at, :] * cl_ref[...] - sh_ref[at, :] * sl_ref[...]
            ).astype(BF)

    def spread(value, out_ref):
        for d in range(n_axial):
            lanes = slice(d * half, (d + 1) * half)
            out_ref[d] = jnp.concatenate([value[:lines, lanes], value[lines:, lanes]], axis=1).astype(BF)

    waves = table[...]
    spread(
        jnp.dot(x_ref[...].reshape(2 * lines, cols), waves, preferred_element_type=F32), px_ref
    )
    for h in range(2):
        for c in range(some):
            slope = gelu_slope(s_ref[h, c].astype(F32))
            grad_ref[h, c] = (c_ref[h, c].astype(F32) * slope).astype(BF)
    spread(
        jnp.dot(grad_ref[...].reshape(2 * lines, cols), waves, preferred_element_type=F32), pg_ref
    )


def radial_matrices(n_radial, rad_rows, rad, group):
    total = n_radial * rad_rows
    shape = (KR * group, group * rad_rows)
    row = lax.broadcasted_iota(jnp.int32, shape, 0)
    col = lax.broadcasted_iota(jnp.int32, shape, 1)
    q = row // group
    freq = q + jnp.where(q >= KR // 2, total - KR, 0)
    point = rad * rad_rows + col % rad_rows
    phase = (freq * point % total).astype(F32) * (2.0 * math.pi / total)
    same = row % group == col // rad_rows
    return jnp.where(same, jnp.cos(phase), 0.0), jnp.where(same, jnp.sin(phase), 0.0)


def comm_kernel(
    n_axial, n_radial, final_scale,
    px_ref, pg_ref, w_hbm, x_hbm, g_hbm, scale_ref,
    spec_ref, gath_ref, wg_ref,
    w_vmem, x_vmem, g_vmem, pair_in, q_buf, chip_in, r_buf, r16, rad_in, dx_all, dx32,
    wl_own, wl_pair, wl_chip, wl_rad, fwd, bwd,
    in_sem, ps, pr, cs, cr, rs, rr, ds_, dr, as_, ar, fs, fr, wps, wpr, wcs, wcr, wrs, wrr,
):
    chips = n_axial // 2
    ax = lax.axis_index("axial")
    rad = lax.axis_index("radial")
    chip = ax // 2
    core = ax % 2
    partner = chip * 2 + 1 - core
    own_k = KA // n_axial
    half = 2 * own_k
    q_own, channels, lanes = spec_ref.shape
    cut = channels // 2
    rad_rows = x_vmem.shape[1]
    cols = x_vmem.shape[2]
    lines = channels * rad_rows
    group = 8
    rows = group * rad_rows
    parts = (pg_ref, px_ref)

    def remote(src, dst, send, recv, where):
        return pltpu.make_async_remote_copy(
            src_ref=src, dst_ref=dst, send_sem=send, recv_sem=recv,
            device_id=where, device_id_type=pl.DeviceIdType.MESH,
        )

    local = [
        pltpu.make_async_copy(x_hbm, x_vmem, in_sem.at[0]),
        pltpu.make_async_copy(g_hbm, g_vmem, in_sem.at[1]),
        pltpu.make_async_copy(w_hbm, w_vmem, in_sem.at[2]),
    ]
    peers = [(chip + t) % chips for t in range(chips)]
    rads = [(rad + t) % n_radial for t in range(n_radial)]
    barrier = pltpu.get_barrier_semaphore()
    greet = [{"axial": partner}]
    greet += [{"axial": peers[t] * 2 + core} for t in range(1, chips)]
    greet += [{"radial": rads[t]} for t in range(1, n_radial)]
    for where in greet:
        pl.semaphore_signal(barrier, inc=1, device_id=where, device_id_type=pl.DeviceIdType.MESH)
    pl.semaphore_wait(barrier, len(greet))

    sent = []
    order = list(range(1, chips)) + [0]
    pair = {}
    for f in range(2):
        for t in order:
            pair[f, t] = remote(
                parts[f].at[peers[t] * 2 + 1 - core], pair_in.at[f, t], ps.at[f, t], pr.at[f, t],
                {"axial": partner},
            )
            pair[f, t].start()
    sent += list(pair.values())
    for copy in local:
        copy.start()
    chip_copies = {}
    for f in range(2):
        for t in order[:-1]:
            pair[f, t].wait_recv()
            q_buf[f, t - 1] = (
                parts[f][peers[t] * 2 + core].astype(F32) + pair_in[f, t].astype(F32)
            ).astype(BF)
            chip_copies[f, t] = remote(
                q_buf.at[f, t - 1], chip_in.at[f, t - 1], cs.at[f, t - 1], cr.at[f, t - 1],
                {"axial": peers[t] * 2 + core},
            )
            chip_copies[f, t].start()
        pair[f, 0].wait_recv()
    sent += list(chip_copies.values())

    cos_m, sin_m = radial_matrices(n_radial, rad_rows, rad, group)
    both = jnp.concatenate([cos_m, sin_m], axis=1)
    high, low = split16(both)
    fwd[...] = jnp.concatenate([high, high, low], axis=1)
    both = jnp.concatenate([cos_m.T, sin_m.T], axis=1)
    high, low = split16(both)
    bwd[...] = jnp.concatenate([high, low], axis=1)

    def transform(f):
        for t in range(1, chips):
            chip_copies[f, t].wait_recv()
        forward = fwd[...]

        for i in range(cut // group):
            at = pl.ds(i * rows, rows)
            z = parts[f][ax, at, :].astype(F32) + pair_in[f, 0, at, :].astype(F32)
            for t in range(chips - 1):
                z = z + chip_in[f, t, at, :].astype(F32)
            turned = jnp.concatenate(
                [z[:, own_k:half], -z[:, :own_k], z[:, half + own_k :], -z[:, half : half + own_k]],
                axis=1,
            )
            zh, zl = split16(z)
            th, tl = split16(turned)
            stack = jnp.concatenate([zh, th, zl, tl, zh, th], axis=0)
            out = jnp.dot(forward, stack, preferred_element_type=F32)
            r_buf[f, :, i * group : (i + 1) * group, :] = out.reshape(KR, group, lanes)
        copies = []
        for t in range(1, n_radial):
            r16[f, t - 1] = r_buf[f, pl.ds(rads[t] * q_own, q_own)].astype(BF)
            copy = remote(
                r16.at[f, t - 1], rad_in.at[f, t - 1], rs.at[f, t - 1], rr.at[f, t - 1],
                {"radial": rads[t]},
            )
            copy.start()
            copies.append(copy)
        return copies

    def collect(f, q):
        value = r_buf[f, rad * q_own + q]
        for t in range(n_radial - 1):
            value = value + rad_in[f, t, q].astype(F32)
        return jnp.concatenate([value[:, :half], value[:, half:]], axis=0)

    rad_g = transform(0)

    local[0].wait()
    local[1].wait()
    piece = 256
    per = piece // rad_rows
    grads = g_vmem[...].reshape(lines, cols)

    def gram(i, carry):
        block = x_vmem[pl.ds(i * per, per)].reshape(piece, cols)
        full = lax.dot_general(block, grads, (((1,), (1,)), ((), ())), preferred_element_type=F32)
        full = full.reshape(per, rad_rows, lines)
        row = lax.broadcasted_iota(jnp.int32, full.shape, 1)
        col = lax.broadcasted_iota(jnp.int32, full.shape, 2) % rad_rows
        picked = jnp.sum(jnp.where(row == col, full, 0.0), axis=1)
        line = lax.broadcasted_iota(jnp.int32, (lines, channels), 0) // rad_rows
        chan = lax.broadcasted_iota(jnp.int32, (lines, channels), 1)
        chooser = jnp.where(line == chan, 1.0, 0.0).astype(F32)
        wl_own[pl.ds(pl.multiple_of(i * per, per), per), :] = jnp.dot(
            picked, chooser, preferred_element_type=F32, precision=lax.Precision.HIGHEST
        )
        return carry

    lax.fori_loop(0, lines // piece, gram, 0)
    wl_first = remote(wl_own, wl_pair, wps, wpr, {"axial": partner})
    wl_first.start()

    rad_x = transform(1)
    sent += rad_g + rad_x + [wl_first]
    wl_first.wait_recv()
    wl_chip[chip] = wl_own[...] + wl_pair[...]
    wl_copies = []
    for t in range(1, chips):
        copy = remote(
            wl_chip.at[chip], wl_chip.at[chip], wcs.at[t - 1], wcr.at[t - 1],
            {"axial": peers[t] * 2 + core},
        )
        copy.start()
        wl_copies.append(copy)
    sent += wl_copies

    local[2].wait()
    for copy in rad_g:
        copy.wait_recv()

    def modes(q, carry):
        g = collect(0, q) * scale_ref[...]
        spec_ref[q, :, half:] = g
        turned = jnp.concatenate([g[:, own_k:], -g[:, :own_k]], axis=1)
        gh, gl = split16(g)
        th, tl = split16(turned)
        side = jnp.concatenate(
            [jnp.concatenate([gh, gl], axis=1), jnp.concatenate([th, tl], axis=1)], axis=0
        )
        out = jnp.dot(
            w_vmem[q].reshape(own_k * channels, 2 * channels), side, preferred_element_type=F32
        )
        lane = lax.broadcasted_iota(jnp.int32, (channels, lanes), 1) % own_k
        total = jnp.zeros((channels, lanes), F32)
        for k in range(own_k):
            total = jnp.where(lane == k, out[k * channels : (k + 1) * channels], total)
        dx = total[:, :half] + total[:, half:]
        dx_all[rad, q] = jnp.concatenate([dx[:cut], dx[cut:]], axis=1).astype(BF)
        return carry

    lax.fori_loop(0, q_own, modes, 0)
    dx_copies = []
    for t in range(1, n_radial):
        copy = remote(dx_all.at[rad], dx_all.at[rad], ds_.at[t - 1], dr.at[t - 1], {"radial": rads[t]})
        copy.start()
        dx_copies.append(copy)
    sent += dx_copies

    for copy in wl_copies:
        copy.wait_recv()
    total = wl_chip[0]
    for t in range(1, chips):
        total = total + wl_chip[t]
    wl_rad[rad] = total
    wl_rad_copies = []
    for t in range(1, n_radial):
        copy = remote(
            wl_rad.at[rad], wl_rad.at[rad], wrs.at[t - 1], wrr.at[t - 1], {"radial": rads[t]}
        )
        copy.start()
        wl_rad_copies.append(copy)
    sent += wl_rad_copies

    for copy in dx_copies:
        copy.wait_recv()
    for t in range(n_radial):
        dx32[t * q_own : (t + 1) * q_own] = dx_all[t].astype(F32)
    backward = bwd[...]
    for i in range(cut // group):
        d = dx32[:, i * group : (i + 1) * group, :].reshape(KR * group, lanes)
        turned = jnp.concatenate(
            [-d[:, own_k:half], d[:, :own_k], -d[:, half + own_k :], d[:, half : half + own_k]], axis=1
        )
        d16 = d.astype(BF)
        t16 = turned.astype(BF)
        stack = jnp.concatenate([d16, t16, d16, t16], axis=0)
        gath_ref[ax, i * rows : (i + 1) * rows, :] = jnp.dot(
            backward, stack, preferred_element_type=F32
        ).astype(BF)
    gather = []
    for t in range(1, chips):
        copy = remote(
            gath_ref.at[ax], gath_ref.at[ax], as_.at[t - 1], ar.at[t - 1], {"axial": peers[t] * 2 + core}
        )
        copy.start()
        gather.append(copy)
    passed = [remote(gath_ref.at[ax], gath_ref.at[ax], fs.at[0], fr.at[0], {"axial": partner})]
    passed[0].start()

    for copy in rad_x:
        copy.wait_recv()

    def keep(q, carry):
        spec_ref[q, :, :half] = collect(1, q)
        return carry

    lax.fori_loop(0, q_own, keep, 0)
    for t in range(1, chips):
        gather[t - 1].wait_recv()
        slot = ((chip - t + chips) % chips) * 2 + core
        copy = remote(gath_ref.at[slot], gath_ref.at[slot], fs.at[t], fr.at[t], {"axial": partner})
        copy.start()
        passed.append(copy)

    for copy in wl_rad_copies:
        copy.wait_recv()
    total = wl_rad[0]
    for t in range(1, n_radial):
        total = total + wl_rad[t]
    wg_ref[...] = total * final_scale

    for copy in passed:
        copy.wait_recv()
    for copy in sent + gather + passed:
        copy.wait_send()


def outer_kernel(own_k, spec_ref, out_ref):
    half = 2 * own_k
    value = spec_ref[0]
    channels = value.shape[0]
    xh, xl = split16(value[:, :half])
    left = jnp.concatenate([xh, xl, xh], axis=1).reshape(channels // 16, 16, 3 * half)
    turned = jnp.transpose(value[:, half:])
    real, imag = turned[:own_k], turned[own_k:]
    sides = jnp.concatenate(
        [jnp.concatenate([real, imag], axis=1), jnp.concatenate([imag, -real], axis=1)], axis=0
    )
    sh, sl = split16(sides)
    right = jnp.concatenate([sh, sh, sl], axis=0)
    lane = lax.broadcasted_iota(jnp.int32, (16, 3 * half), 1) % own_k
    together = 8
    for first in range(0, own_k, together):
        rows = []
        for k in range(first, first + together):
            mask = jnp.where(lane == k, 1.0, 0.0).astype(BF)
            rows.append((left * mask[None]).reshape(channels, 3 * half))
        out = jnp.dot(jnp.concatenate(rows, axis=0), right, preferred_element_type=F32)
        out_ref[0, first : first + together] = out.reshape(together, channels, 2 * channels)


def final_kernel(
    n_axial, pw_ref, grad_ref, cl_ref, sl_ref, ch_ref, sh_ref, gath_ref, out_ref, left, table
):
    channels, rad_rows, cols = grad_ref.shape
    lines = channels * rad_rows
    half = 2 * KA // n_axial
    pieces = table.shape[1] // LANES
    step = pl.program_id(0)

    @pl.when(step == 0)
    def _():
        line = lax.broadcasted_iota(jnp.int32, (lines, channels), 0) // rad_rows
        chan = lax.broadcasted_iota(jnp.int32, (lines, channels), 1)
        chooser = jnp.where(line == chan, 1.0, 0.0).astype(BF)
        rows = jnp.dot(chooser, pw_ref[...], preferred_element_type=F32).astype(BF)
        dims = (((1,), (1,)), ((), ()))
        wide = lax.dot_general(rows, chooser, dims, preferred_element_type=F32)
        row = lax.broadcasted_iota(jnp.int32, wide.shape, 0) % rad_rows
        col = lax.broadcasted_iota(jnp.int32, wide.shape, 1) % rad_rows
        left[:, :lines] = jnp.where(row == col, wide, 0.0).astype(BF)
        cut = lines // 2
        for d in range(n_axial):
            lanes = slice(lines + d * half, lines + (d + 1) * half)
            left[:cut, lanes] = gath_ref[d, :, :half]
            left[cut:, lanes] = gath_ref[d, :, half:]
        first = pl.multiple_of(lax.axis_index("axial") * pieces, pieces)
        cos_high = jnp.transpose(ch_ref[pl.ds(first, pieces), :])
        sin_high = jnp.transpose(sh_ref[pl.ds(first, pieces), :])
        for u in range(pieces):
            table[:, u * LANES : (u + 1) * LANES] = (
                cos_high[:, u : u + 1] * cl_ref[...] - sin_high[:, u : u + 1] * sl_ref[...]
            ).astype(BF)

    waves = table[:, pl.ds(pl.multiple_of(step * cols, cols), cols)]
    right = jnp.concatenate([grad_ref[...].reshape(lines, cols), waves], axis=0)
    value = jnp.dot(left[...], right, preferred_element_type=F32)
    out_ref[...] = value.astype(BF).reshape(channels, rad_rows, cols)


def params(**more):
    return pltpu.CompilerParams(vmem_limit_bytes=VMEM_LIMIT, **more)


def body(inputs, saved_pre, cotangent, pointwise_weight, spectral_weight):
    channels, rad_rows, ax_cols = inputs.shape
    n_axial = lax.axis_size("axial")
    n_radial = lax.axis_size("radial")
    ax_index = lax.axis_index("axial")
    points = ax_cols * n_axial * rad_rows * n_radial
    own_k = KA // n_axial
    q_own = KR // n_radial
    lines = channels * rad_rows
    lanes = 4 * own_k
    chips = n_axial // 2
    cut = channels // 2

    cos_low, sin_low, cos_high, sin_high = axial_factors(n_axial, ax_cols)
    orders = ax_index * own_k + jnp.arange(own_k, dtype=jnp.int32)
    weights = jnp.where(orders == 0, 1.0, 2.0).astype(F32) / points
    scale = jnp.concatenate([weights, weights]).reshape(1, 2 * own_k)

    whole = lambda *shape: pl.BlockSpec(shape, lambda i: (0,) * len(shape))
    group = 8
    field = pl.BlockSpec((2, group, rad_rows, ax_cols), lambda i: (0, i, 0, 0))
    halves = lambda value: value.reshape(2, cut, rad_rows, ax_cols)
    part = pl.BlockSpec((n_axial, group * rad_rows, lanes), lambda i: (0, i, 0))
    part_shape = jax.ShapeDtypeStruct((n_axial, lines // 2, lanes), BF)
    part_x, part_g, grad_pre = pl.pallas_call(
        functools.partial(local_kernel, n_axial),
        grid=(cut // group,),
        in_specs=[
            field, field, field,
            whole(*cos_low.shape), whole(*cos_low.shape), whole(*cos_high.shape), whole(*cos_high.shape),
        ],
        out_specs=[part, part, field],
        out_shape=[
            part_shape,
            part_shape,
            jax.ShapeDtypeStruct((2, cut, rad_rows, ax_cols), BF),
        ],
        scratch_shapes=[pltpu.VMEM((ax_cols, 2 * KA), BF)],
        compiler_params=params(),
        name="local_transform",
    )(halves(inputs), halves(saved_pre), halves(cotangent), cos_low, sin_low, cos_high, sin_high)
    grad_pre = grad_pre.reshape(channels, rad_rows, ax_cols)

    vmem = pl.BlockSpec(memory_space=pltpu.VMEM)
    hbm = pl.BlockSpec(memory_space=pl.ANY)
    dma = lambda *count: pltpu.SemaphoreType.DMA(count)
    one = pltpu.SemaphoreType.DMA
    spec, gathered, weight_grad = pl.pallas_call(
        functools.partial(comm_kernel, n_axial, n_radial, 1.0 / math.sqrt(points)),
        in_specs=[vmem, vmem, hbm, hbm, hbm, vmem],
        out_specs=[vmem, vmem, vmem],
        out_shape=[
            jax.ShapeDtypeStruct((q_own, channels, lanes), F32),
            jax.ShapeDtypeStruct((n_axial, lines // 2, lanes), BF),
            jax.ShapeDtypeStruct((channels, channels), F32),
        ],
        scratch_shapes=[
            pltpu.VMEM(spectral_weight.shape, BF),
            pltpu.VMEM(inputs.shape, BF),
            pltpu.VMEM(inputs.shape, BF),
            pltpu.VMEM((2, chips, lines // 2, lanes), BF),
            pltpu.VMEM((2, chips - 1, lines // 2, lanes), BF),
            pltpu.VMEM((2, chips - 1, lines // 2, lanes), BF),
            pltpu.VMEM((2, KR, cut, lanes), F32),
            pltpu.VMEM((2, n_radial - 1, q_own, cut, lanes), BF),
            pltpu.VMEM((2, n_radial - 1, q_own, cut, lanes), BF),
            pltpu.VMEM((n_radial, q_own, cut, lanes), BF),
            pltpu.VMEM((KR, cut, lanes), F32),
            pltpu.VMEM((channels, channels), F32),
            pltpu.VMEM((channels, channels), F32),
            pltpu.VMEM((chips, channels, channels), F32),
            pltpu.VMEM((n_radial, channels, channels), F32),
            pltpu.VMEM((KR * group, 6 * group * rad_rows), BF),
            pltpu.VMEM((group * rad_rows, 4 * KR * group), BF),
            dma(3),
            dma(2, chips), dma(2, chips),
            dma(2, chips - 1), dma(2, chips - 1),
            dma(2, n_radial - 1), dma(2, n_radial - 1),
            dma(n_radial - 1), dma(n_radial - 1),
            dma(chips - 1), dma(chips - 1),
            dma(chips), dma(chips),
            one, one,
            dma(chips - 1), dma(chips - 1),
            dma(n_radial - 1), dma(n_radial - 1),
        ],
        compiler_params=params(collective_id=0, has_side_effects=True),
        name="exchange",
    )(part_x, part_g, spectral_weight, inputs, grad_pre, scale)

    spectral_grad = pl.pallas_call(
        functools.partial(outer_kernel, own_k),
        grid=(q_own,),
        in_specs=[pl.BlockSpec((1, channels, lanes), lambda i: (i, 0, 0))],
        out_specs=pl.BlockSpec((1, own_k, channels, 2 * channels), lambda i: (i, 0, 0, 0)),
        out_shape=jax.ShapeDtypeStruct((q_own, own_k, channels, 2 * channels), F32),
        compiler_params=params(),
        name="mode_products",
    )(spec)

    steps = 4
    cols = ax_cols // steps
    strip = pl.BlockSpec((channels, rad_rows, cols), lambda i: (0, 0, i))
    flip = lambda value: np.ascontiguousarray(value.T)
    input_grad = pl.pallas_call(
        functools.partial(final_kernel, n_axial),
        grid=(steps,),
        in_specs=[
            whole(channels, channels),
            strip,
            whole(2 * KA, LANES), whole(2 * KA, LANES),
            whole(*cos_high.shape), whole(*cos_high.shape),
            whole(n_axial, lines // 2, lanes),
        ],
        out_specs=strip,
        out_shape=jax.ShapeDtypeStruct((channels, rad_rows, ax_cols), BF),
        scratch_shapes=[
            pltpu.VMEM((lines, lines + 2 * KA), BF),
            pltpu.VMEM((2 * KA, ax_cols), BF),
        ],
        compiler_params=params(),
        name="input_gradient",
    )(pointwise_weight, grad_pre, flip(cos_low), flip(sin_low), cos_high, sin_high, gathered)
    return (input_grad, spectral_grad, weight_grad)


def solution(mesh):
    field = P(None, "radial", ("parts", "axial"))
    return jax.shard_map(
        body,
        mesh=mesh,
        in_specs=(field, field, field, P(), P("radial", "axial", None, None)),
        out_specs=(field, P("radial", ("parts", "axial"), None, None), P("parts", None)),
        check_vma=False,
    )
```

time: 316 us -> 73.4 us (0.23)
  the two profiles are of different devices: /device:TPU:0 before, /device:TPU:25 now
where the time goes in v1:
time: 73.4 us; the launch traced here: 72.7 us
  Pallas kernels  70.8 us (96%)
    pallas_call x1, Pallas kernels, body(): pl.pallas_call(functools.partial(comm_kernel, n_axial, n_radial, 1.0 / ma...  46.4 us
    pallas_call x1, Pallas kernels, body(): pl.pallas_call(functools.partial(final_kernel, n_axial), grid=(steps,), i...  8.64 us
    pallas_call x1, Pallas kernels, body(): pl.pallas_call(functools.partial(outer_kernel, own_k), grid=(q_own,), in_...  8 us
    pallas_call x1, Pallas kernels, body(): pl.pallas_call(functools.partial(local_kernel, n_axial), grid=(cut // gro...  7.8 us

profile of v1, /device:TPU:25, one launch (start us, length us, event | category | flops | bytes accessed | tf_op | source)
XLA Modules:
  0.0 72.7 jit_solution(13813052492051419381)
XLA Ops:
  0.6 0.6 maximum_bitcast_fusion.scale_ref
  1.2 7.8 %local_transform.1 = (bf16[8,512,128]{2,1,0:T(8,128)(2,1)}, bf16[8,512,128]{2,1,0:T(8,128)(2,1)}, bf16[2,32,16,1024]{3,2,1,0:T(8,128)(2,1)}) custom-call(bf16[2,32,16,1024]{3,2,1,0:T(8,128)(2,1)} %bitcast.6, bf16[2,32,16,1024]{3,2,1,0:T(8,128)(2,1)} %bitcast.9, bf16[2,32,16,1024]{3,2,1,0:T(8,128)(2,1)} %bitcast.10, f32[128,512]{1,0:T(8,128)} %constant.29.clone.cl_ref, ...), custom_call_target="tpu_custom_call" | custom-call | tf_op jit(solution)/shard_map/local_transform/pallas_call | solution.py:445
  9.0 46.4 %exchange.1 = (f32[8,64,128]{2,1,0:T(8,128)}, bf16[8,512,128]{2,1,0:T(8,128)(2,1)}, f32[64,64]{1,0:T(8,128)}) custom-call(bf16[8,512,128]{2,1,0:T(8,128)(2,1)} %get-tuple-element.10.px_ref, bf16[8,512,128]{2,1,0:T(8,128)(2,1)} %get-tuple-element.11.pg_ref, bf16[8,32,64,128]{3,2,1,0:T(8,128)(2,1)} %w_hbm.1, bf16[64,16,1024]{2,1,0:T(8,128)(2,1)} %x_hbm.1, ...), custom_call_target="tpu_custom_call" | custom-call | tf_op jit(solution)/shard_map/exchange/pallas_call | solution.py:468
  55.4 8.6 %input_gradient.1 = bf16[64,16,1024]{2,1,0:T(8,128)(2,1)} custom-call(bf16[64,64]{1,0:T(8,128)(2,1)} %pw_ref.1, bf16[64,16,1024]{2,1,0:T(8,128)(2,1)} %bitcast.8, f32[512,128]{1,0:T(8,128)} %constant.33.clone.cl_ref, f32[512,128]{1,0:T(8,128)} %constant.34.clone.sl_ref, f32[64,512]{1,0:T(8,128)} %constant.31.clone.ch_ref, f32[64,512]{1,0:T(8,128)} %constant.32.clone.sh_ref, ...), custom_call_target="tpu_custom_call" | custom-call | tf_op jit(solution)/shard_map/input_gradient/pallas_call | solution.py:524
  64.1 0.0 copy-start
  64.1 8.0 %mode_products.1 = f32[8,32,64,128]{3,2,1,0:T(8,128)} custom-call(f32[8,64,128]{2,1,0:T(8,128)} %get-tuple-element.13.spec_ref), custom_call_target="tpu_custom_call" | custom-call | tf_op jit(solution)/shard_map/mode_products/pallas_call | solution.py:510
  72.1 0.0 copy-done
  72.1 0.6 copy.15
  (1 shorter events, 0.0 us)
Async XLA Ops:
  64.1 8.0 %copy-start = (f32[64,64]{1,0:T(8,128)S(1)}, f32[64,64]{1,0:T(8,128)}, u32[]{:S(2)}) copy-start(f32[64,64]{1,0:T(8,128)} %get-tuple-element.20) | copy-start | bytes 49156

commit v2 on v1

--- a/solution.py
+++ b/solution.py
@@ -43,41 +43,6 @@
     ) * (1.0 / math.sqrt(2.0 * math.pi))
 
 
-def local_kernel(
-    n_axial, x_ref, s_ref, c_ref, cl_ref, sl_ref, ch_ref, sh_ref, px_ref, pg_ref, grad_ref, table
-):
-    _, some, rad_rows, cols = x_ref.shape
-    lines = some * rad_rows
-    half = 2 * KA // n_axial
-    pieces = cols // LANES
-
-    @pl.when(pl.program_id(0) == 0)
-    def _():
-        first = lax.axis_index("axial") * pieces
-        for u in range(pieces):
-            at = pl.ds(first + u, 1)
-            table[u * LANES : (u + 1) * LANES, :] = (
-                ch_ref[at, :] * cl_ref[...] - sh_ref[at, :] * sl_ref[...]
-            ).astype(BF)
-
-    def spread(value, out_ref):
-        for d in range(n_axial):
-            lanes = slice(d * half, (d + 1) * half)
-            out_ref[d] = jnp.concatenate([value[:lines, lanes], value[lines:, lanes]], axis=1).astype(BF)
-
-    waves = table[...]
-    spread(
-        jnp.dot(x_ref[...].reshape(2 * lines, cols), waves, preferred_element_type=F32), px_ref
-    )
-    for h in range(2):
-        for c in range(some):
-            slope = gelu_slope(s_ref[h, c].astype(F32))
-            grad_ref[h, c] = (c_ref[h, c].astype(F32) * slope).astype(BF)
-    spread(
-        jnp.dot(grad_ref[...].reshape(2 * lines, cols), waves, preferred_element_type=F32), pg_ref
-    )
-
-
 def radial_matrices(n_radial, rad_rows, rad, group):
     total = n_radial * rad_rows
     shape = (KR * group, group * rad_rows)
@@ -93,11 +58,11 @@
 
 def comm_kernel(
     n_axial, n_radial, final_scale,
-    px_ref, pg_ref, w_hbm, x_hbm, g_hbm, scale_ref,
-    spec_ref, gath_ref, wg_ref,
-    w_vmem, x_vmem, g_vmem, pair_in, q_buf, chip_in, r_buf, r16, rad_in, dx_all, dx32,
+    w_hbm, x_hbm, s_hbm, c_hbm, cl_ref, sl_ref, ch_ref, sh_ref,
+    spec_ref, gath_ref, wg_ref, g_hbm,
+    w_vmem, x_vmem, s_vmem, c_vmem, g_vmem, table, px_ref, pg_ref, pair_in, q_buf, chip_in, r_buf, r16, rad_in, dx_all, dx32,
     wl_own, wl_pair, wl_chip, wl_rad, fwd, bwd,
-    in_sem, ps, pr, cs, cr, rs, rr, ds_, dr, as_, ar, fs, fr, wps, wpr, wcs, wcr, wrs, wrr,
+    in_sem, out_sem, s_sem, c_sem, ps, pr, cs, cr, rs, rr, ds_, dr, as_, ar, fs, fr, wps, wpr, wcs, wcr, wrs, wrr,
 ):
     chips = n_axial // 2
     ax = lax.axis_index("axial")
@@ -109,8 +74,8 @@
     half = 2 * own_k
     q_own, channels, lanes = spec_ref.shape
     cut = channels // 2
-    rad_rows = x_vmem.shape[1]
-    cols = x_vmem.shape[2]
+    rad_rows, cols = x_vmem.shape[2:]
+    points = n_axial * n_radial * rad_rows * cols
     lines = channels * rad_rows
     group = 8
     rows = group * rad_rows
@@ -122,11 +87,24 @@
             device_id=where, device_id_type=pl.DeviceIdType.MESH,
         )
 
+    blocks = cut // group
+    loads = []
+    for i in range(blocks):
+        at = pl.ds(i * group, group)
+        loads.append(
+            (
+                pltpu.make_async_copy(s_hbm.at[:, at], s_vmem.at[:, at], s_sem.at[i]),
+                pltpu.make_async_copy(c_hbm.at[:, at], c_vmem.at[:, at], c_sem.at[i]),
+            )
+        )
+        for copy in loads[-1]:
+            copy.start()
     local = [
         pltpu.make_async_copy(x_hbm, x_vmem, in_sem.at[0]),
-        pltpu.make_async_copy(g_hbm, g_vmem, in_sem.at[1]),
-        pltpu.make_async_copy(w_hbm, w_vmem, in_sem.at[2]),
+        pltpu.make_async_copy(w_hbm, w_vmem, in_sem.at[1]),
     ]
+    for copy in local:
+        copy.start()
     peers = [(chip + t) % chips for t in range(chips)]
     rads = [(rad + t) % n_radial for t in range(n_radial)]
     barrier = pltpu.get_barrier_semaphore()
@@ -135,23 +113,58 @@
     greet += [{"radial": rads[t]} for t in range(1, n_radial)]
     for where in greet:
         pl.semaphore_signal(barrier, inc=1, device_id=where, device_id_type=pl.DeviceIdType.MESH)
+
+    pieces = cols // LANES
+    for u in range(pieces):
+        at = pl.ds(ax * pieces + u, 1)
+        table[u * LANES : (u + 1) * LANES, :] = (
+            ch_ref[at, :] * cl_ref[...] - sh_ref[at, :] * sl_ref[...]
+        ).astype(BF)
+    cos_m, sin_m = radial_matrices(n_radial, rad_rows, rad, group)
+    both = jnp.concatenate([cos_m, sin_m], axis=1)
+    high, low = split16(both)
+    fwd[...] = jnp.concatenate([high, high, low], axis=1)
+    both = jnp.concatenate([cos_m.T, sin_m.T], axis=1)
+    high, low = split16(both)
+    bwd[...] = jnp.concatenate([high, low], axis=1)
+    waves = table[...]
+
+    def spread(field, out_ref, i):
+        block = field[:, i * group : (i + 1) * group].reshape(2 * rows, cols)
+        value = jnp.dot(block, waves, preferred_element_type=F32)
+        for d in range(n_axial):
+            at = slice(d * half, (d + 1) * half)
+            out_ref[d, i * rows : (i + 1) * rows, :] = jnp.concatenate(
+                [value[:rows, at], value[rows:, at]], axis=1
+            ).astype(BF)
+
+    for i in range(blocks):
+        for copy in loads[i]:
+            copy.wait()
+        at = slice(i * group, (i + 1) * group)
+        for h in range(2):
+            slope = gelu_slope(s_vmem[h, at].astype(F32))
+            g_vmem[h, at] = (c_vmem[h, at].astype(F32) * slope).astype(BF)
+        spread(g_vmem, pg_ref, i)
+    grad_copy = pltpu.make_async_copy(g_vmem, g_hbm, out_sem)
+    grad_copy.start()
     pl.semaphore_wait(barrier, len(greet))
 
     sent = []
     order = list(range(1, chips)) + [0]
     pair = {}
+    chip_copies = {}
     for f in range(2):
+        if f == 1:
+            local[0].wait()
+            for i in range(blocks):
+                spread(x_vmem, px_ref, i)
         for t in order:
             pair[f, t] = remote(
                 parts[f].at[peers[t] * 2 + 1 - core], pair_in.at[f, t], ps.at[f, t], pr.at[f, t],
                 {"axial": partner},
             )
             pair[f, t].start()
-    sent += list(pair.values())
-    for copy in local:
-        copy.start()
-    chip_copies = {}
-    for f in range(2):
         for t in order[:-1]:
             pair[f, t].wait_recv()
             q_buf[f, t - 1] = (
@@ -163,15 +176,7 @@
             )
             chip_copies[f, t].start()
         pair[f, 0].wait_recv()
-    sent += list(chip_copies.values())
-
-    cos_m, sin_m = radial_matrices(n_radial, rad_rows, rad, group)
-    both = jnp.concatenate([cos_m, sin_m], axis=1)
-    high, low = split16(both)
-    fwd[...] = jnp.concatenate([high, high, low], axis=1)
-    both = jnp.concatenate([cos_m.T, sin_m.T], axis=1)
-    high, low = split16(both)
-    bwd[...] = jnp.concatenate([high, low], axis=1)
+    sent += list(pair.values()) + list(chip_copies.values())
 
     def transform(f):
         for t in range(1, chips):
@@ -211,14 +216,12 @@
 
     rad_g = transform(0)
 
-    local[0].wait()
-    local[1].wait()
     piece = 256
     per = piece // rad_rows
     grads = g_vmem[...].reshape(lines, cols)
 
     def gram(i, carry):
-        block = x_vmem[pl.ds(i * per, per)].reshape(piece, cols)
+        block = x_vmem[i // (cut // per), pl.ds(i % (cut // per) * per, per)].reshape(piece, cols)
         full = lax.dot_general(block, grads, (((1,), (1,)), ((), ())), preferred_element_type=F32)
         full = full.reshape(per, rad_rows, lines)
         row = lax.broadcasted_iota(jnp.int32, full.shape, 1)
@@ -250,12 +253,15 @@
         wl_copies.append(copy)
     sent += wl_copies
 
-    local[2].wait()
+    local[1].wait()
     for copy in rad_g:
         copy.wait_recv()
 
+    mode = lax.broadcasted_iota(jnp.int32, (channels, half), 1) % own_k + ax * own_k
+    scale = jnp.where(mode == 0, 1.0 / points, 2.0 / points)
+
     def modes(q, carry):
-        g = collect(0, q) * scale_ref[...]
+        g = collect(0, q) * scale
         spec_ref[q, :, half:] = g
         turned = jnp.concatenate([g[:, own_k:], -g[:, :own_k]], axis=1)
         gh, gl = split16(g)
@@ -349,11 +355,11 @@
         copy.wait_recv()
     for copy in sent + gather + passed:
         copy.wait_send()
-
-
-def outer_kernel(own_k, spec_ref, out_ref):
+    grad_copy.wait()
+
+
+def mode_products(own_k, value, out_ref):
     half = 2 * own_k
-    value = spec_ref[0]
     channels = value.shape[0]
     xh, xl = split16(value[:, :half])
     left = jnp.concatenate([xh, xl, xh], axis=1).reshape(channels // 16, 16, 3 * half)
@@ -372,20 +378,32 @@
             mask = jnp.where(lane == k, 1.0, 0.0).astype(BF)
             rows.append((left * mask[None]).reshape(channels, 3 * half))
         out = jnp.dot(jnp.concatenate(rows, axis=0), right, preferred_element_type=F32)
-        out_ref[0, first : first + together] = out.reshape(together, channels, 2 * channels)
+        out_ref[first : first + together] = out.reshape(together, channels, 2 * channels)
 
 
 def final_kernel(
-    n_axial, pw_ref, grad_ref, cl_ref, sl_ref, ch_ref, sh_ref, gath_ref, out_ref, left, table
+    n_axial, pw_ref, grad_ref, cl_ref, sl_ref, ch_ref, sh_ref, gath_ref, spec_ref, wg_ref,
+    out_ref, modes_hbm, wg_out, left, table, modes_vmem, mode_sem,
 ):
     channels, rad_rows, cols = grad_ref.shape
     lines = channels * rad_rows
     half = 2 * KA // n_axial
     pieces = table.shape[1] // LANES
     step = pl.program_id(0)
+    q_own = spec_ref.shape[0]
+
+    def store(q):
+        return pltpu.make_async_copy(modes_vmem.at[q], modes_hbm.at[q], mode_sem.at[q])
 
     @pl.when(step == 0)
     def _():
+        def products(q, carry):
+            mode_products(KA // n_axial, spec_ref[q], modes_vmem.at[q])
+            store(q).start()
+            return carry
+
+        lax.fori_loop(0, q_own, products, 0)
+        wg_out[...] = wg_ref[...]
         line = lax.broadcasted_iota(jnp.int32, (lines, channels), 0) // rad_rows
         chan = lax.broadcasted_iota(jnp.int32, (lines, channels), 1)
         chooser = jnp.where(line == chan, 1.0, 0.0).astype(BF)
@@ -413,6 +431,11 @@
     value = jnp.dot(left[...], right, preferred_element_type=F32)
     out_ref[...] = value.astype(BF).reshape(channels, rad_rows, cols)
 
+    @pl.when(step == pl.num_programs(0) - 1)
+    def _():
+        for q in range(q_own):
+            store(q).wait()
+
 
 def params(**more):
     return pltpu.CompilerParams(vmem_limit_bytes=VMEM_LIMIT, **more)
@@ -422,7 +445,6 @@
     channels, rad_rows, ax_cols = inputs.shape
     n_axial = lax.axis_size("axial")
     n_radial = lax.axis_size("radial")
-    ax_index = lax.axis_index("axial")
     points = ax_cols * n_axial * rad_rows * n_radial
     own_k = KA // n_axial
     q_own = KR // n_radial
@@ -432,52 +454,33 @@
     cut = channels // 2
 
     cos_low, sin_low, cos_high, sin_high = axial_factors(n_axial, ax_cols)
-    orders = ax_index * own_k + jnp.arange(own_k, dtype=jnp.int32)
-    weights = jnp.where(orders == 0, 1.0, 2.0).astype(F32) / points
-    scale = jnp.concatenate([weights, weights]).reshape(1, 2 * own_k)
-
     whole = lambda *shape: pl.BlockSpec(shape, lambda i: (0,) * len(shape))
     group = 8
-    field = pl.BlockSpec((2, group, rad_rows, ax_cols), lambda i: (0, i, 0, 0))
     halves = lambda value: value.reshape(2, cut, rad_rows, ax_cols)
-    part = pl.BlockSpec((n_axial, group * rad_rows, lanes), lambda i: (0, i, 0))
-    part_shape = jax.ShapeDtypeStruct((n_axial, lines // 2, lanes), BF)
-    part_x, part_g, grad_pre = pl.pallas_call(
-        functools.partial(local_kernel, n_axial),
-        grid=(cut // group,),
-        in_specs=[
-            field, field, field,
-            whole(*cos_low.shape), whole(*cos_low.shape), whole(*cos_high.shape), whole(*cos_high.shape),
-        ],
-        out_specs=[part, part, field],
-        out_shape=[
-            part_shape,
-            part_shape,
-            jax.ShapeDtypeStruct((2, cut, rad_rows, ax_cols), BF),
-        ],
-        scratch_shapes=[pltpu.VMEM((ax_cols, 2 * KA), BF)],
-        compiler_params=params(),
-        name="local_transform",
-    )(halves(inputs), halves(saved_pre), halves(cotangent), cos_low, sin_low, cos_high, sin_high)
-    grad_pre = grad_pre.reshape(channels, rad_rows, ax_cols)
-
+    split = (2, cut, rad_rows, ax_cols)
     vmem = pl.BlockSpec(memory_space=pltpu.VMEM)
     hbm = pl.BlockSpec(memory_space=pl.ANY)
     dma = lambda *count: pltpu.SemaphoreType.DMA(count)
     one = pltpu.SemaphoreType.DMA
-    spec, gathered, weight_grad = pl.pallas_call(
+    spec, gathered, weight_grad, grad_pre = pl.pallas_call(
         functools.partial(comm_kernel, n_axial, n_radial, 1.0 / math.sqrt(points)),
-        in_specs=[vmem, vmem, hbm, hbm, hbm, vmem],
-        out_specs=[vmem, vmem, vmem],
+        in_specs=[hbm, hbm, hbm, hbm, vmem, vmem, vmem, vmem],
+        out_specs=[vmem, vmem, vmem, hbm],
         out_shape=[
             jax.ShapeDtypeStruct((q_own, channels, lanes), F32),
             jax.ShapeDtypeStruct((n_axial, lines // 2, lanes), BF),
             jax.ShapeDtypeStruct((channels, channels), F32),
+            jax.ShapeDtypeStruct(split, BF),
         ],
         scratch_shapes=[
             pltpu.VMEM(spectral_weight.shape, BF),
-            pltpu.VMEM(inputs.shape, BF),
-            pltpu.VMEM(inputs.shape, BF),
+            pltpu.VMEM(split, BF),
+            pltpu.VMEM(split, BF),
+            pltpu.VMEM(split, BF),
+            pltpu.VMEM(split, BF),
+            pltpu.VMEM((ax_cols, 2 * KA), BF),
+            pltpu.VMEM((n_axial, lines // 2, lanes), BF),
+            pltpu.VMEM((n_axial, lines // 2, lanes), BF),
             pltpu.VMEM((2, chips, lines // 2, lanes), BF),
             pltpu.VMEM((2, chips - 1, lines // 2, lanes), BF),
             pltpu.VMEM((2, chips - 1, lines // 2, lanes), BF),
@@ -492,7 +495,7 @@
             pltpu.VMEM((n_radial, channels, channels), F32),
             pltpu.VMEM((KR * group, 6 * group * rad_rows), BF),
             pltpu.VMEM((group * rad_rows, 4 * KR * group), BF),
-            dma(3),
+            dma(2), one, dma(cut // group), dma(cut // group),
             dma(2, chips), dma(2, chips),
             dma(2, chips - 1), dma(2, chips - 1),
             dma(2, n_radial - 1), dma(2, n_radial - 1),
@@ -505,23 +508,17 @@
         ],
         compiler_params=params(collective_id=0, has_side_effects=True),
         name="exchange",
-    )(part_x, part_g, spectral_weight, inputs, grad_pre, scale)
-
-    spectral_grad = pl.pallas_call(
-        functools.partial(outer_kernel, own_k),
-        grid=(q_own,),
-        in_specs=[pl.BlockSpec((1, channels, lanes), lambda i: (i, 0, 0))],
-        out_specs=pl.BlockSpec((1, own_k, channels, 2 * channels), lambda i: (i, 0, 0, 0)),
-        out_shape=jax.ShapeDtypeStruct((q_own, own_k, channels, 2 * channels), F32),
-        compiler_params=params(),
-        name="mode_products",
-    )(spec)
+    )(
+        spectral_weight, halves(inputs), halves(saved_pre), halves(cotangent),
+        cos_low, sin_low, cos_high, sin_high,
+    )
+    grad_pre = grad_pre.reshape(channels, rad_rows, ax_cols)
 
     steps = 4
     cols = ax_cols // steps
     strip = pl.BlockSpec((channels, rad_rows, cols), lambda i: (0, 0, i))
     flip = lambda value: np.ascontiguousarray(value.T)
-    input_grad = pl.pallas_call(
+    input_grad, spectral_grad, weight_grad = pl.pallas_call(
         functools.partial(final_kernel, n_axial),
         grid=(steps,),
         in_specs=[
@@ -530,16 +527,24 @@
             whole(2 * KA, LANES), whole(2 * KA, LANES),
             whole(*cos_high.shape), whole(*cos_high.shape),
             whole(n_axial, lines // 2, lanes),
+            whole(q_own, channels, lanes),
+            whole(channels, channels),
         ],
-        out_specs=strip,
-        out_shape=jax.ShapeDtypeStruct((channels, rad_rows, ax_cols), BF),
+        out_specs=[strip, hbm, whole(channels, channels)],
+        out_shape=[
+            jax.ShapeDtypeStruct((channels, rad_rows, ax_cols), BF),
+            jax.ShapeDtypeStruct((q_own, own_k, channels, 2 * channels), F32),
+            jax.ShapeDtypeStruct((channels, channels), F32),
+        ],
         scratch_shapes=[
             pltpu.VMEM((lines, lines + 2 * KA), BF),
             pltpu.VMEM((2 * KA, ax_cols), BF),
+            pltpu.VMEM((q_own, own_k, channels, 2 * channels), F32),
+            dma(q_own),
         ],
         compiler_params=params(),
         name="input_gradient",
-    )(pointwise_weight, grad_pre, flip(cos_low), flip(sin_low), cos_high, sin_high, gathered)
+    )(pointwise_weight, grad_pre, flip(cos_low), flip(sin_low), cos_high, sin_high, gathered, spec, weight_grad)
     return (input_grad, spectral_grad, weight_grad)
 
 

time: 73.4 us -> 62 us (0.84)
  Pallas kernels: 70.8 us -> 60.9 us
    pallas_call x2 -> x0, Pallas kernels: 15.8 us -> none  [the longest x1 8 us: body(): pl.pallas_call(functools.partial(outer_kernel, own_k), grid=(q_own,), in_...]
    pallas_call x1, Pallas kernels: 8.64 us -> 14 us  [body(): pl.pallas_call(functools.partial(final_kernel, n_axial), grid=(steps,), i...]
where the time goes in v2:
time: 62 us; the launch traced here: 61.5 us
  Pallas kernels  60.9 us (98%)
  between operations  0.64 us (1%)
    pallas_call x1, Pallas kernels, body(): pl.pallas_call(functools.partial(comm_kernel, n_axial, n_radial, 1.0 / ma...  46.9 us
    pallas_call x1, Pallas kernels, body(): pl.pallas_call(functools.partial(final_kernel, n_axial), grid=(steps,), i...  14 us

profile of v2, /device:TPU:25, one launch (start us, length us, event | category | flops | bytes accessed | tf_op | source)
XLA Modules:
  0.0 61.5 jit_solution(8878749841148660710)
XLA Ops:
  0.6 46.9 %exchange.1 = (f32[8,64,128]{2,1,0:T(8,128)}, bf16[8,512,128]{2,1,0:T(8,128)(2,1)}, f32[64,64]{1,0:T(8,128)}, bf16[2,32,16,1024]{3,2,1,0:T(8,128)(2,1)}) custom-call(bf16[8,32,64,128]{3,2,1,0:T(8,128)(2,1)} %w_hbm.1, bf16[2,32,16,1024]{3,2,1,0:T(8,128)(2,1)} %bitcast.5, bf16[2,32,16,1024]{3,2,1,0:T(8,128)(2,1)} %bitcast.6, ...), custom_call_target="tpu_custom_call" | custom-call | tf_op jit(solution)/shard_map/exchange/pallas_call | solution.py:465
  47.6 14.0 %input_gradient.1 = (bf16[64,16,1024]{2,1,0:T(8,128)(2,1)}, f32[8,32,64,128]{3,2,1,0:T(8,128)}, f32[64,64]{1,0:T(8,128)}) custom-call(bf16[64,64]{1,0:T(8,128)(2,1)} %pw_ref.1, bf16[64,16,1024]{2,1,0:T(8,128)(2,1)} %bitcast.4, f32[512,128]{1,0:T(8,128)} %constant.16.clone.cl_ref, f32[512,128]{1,0:T(8,128)} %constant.17.clone.sl_ref, ...), custom_call_target="tpu_custom_call" | custom-call | tf_op jit(solution)/shard_map/input_gradient/pallas_call | solution.py:521

commit v3 on v2

--- a/solution.py
+++ b/solution.py
@@ -32,6 +32,25 @@
     return as32(np.cos(low)), as32(np.sin(low)), as32(np.cos(high)), as32(np.sin(high))
 
 
+def rest_of(value, size):
+    return value & (size - 1) if size & (size - 1) == 0 else value % size
+
+
+def part_of(value, size):
+    return value >> (size.bit_length() - 1) if size & (size - 1) == 0 else value // size
+
+
+def same_row(rad_rows, lines):
+    row = lax.broadcasted_iota(jnp.int32, (rad_rows, lines), 0)
+    return row == rest_of(lax.broadcasted_iota(jnp.int32, (rad_rows, lines), 1), rad_rows)
+
+
+def chooser_of(lines, channels, rad_rows, kind):
+    line = part_of(lax.broadcasted_iota(jnp.int32, (lines, channels), 0), rad_rows)
+    chan = lax.broadcasted_iota(jnp.int32, (lines, channels), 1)
+    return jnp.where(line == chan, 1.0, 0.0).astype(kind)
+
+
 def split16(value):
     high = value.astype(BF)
     return high, (value - high.astype(F32)).astype(BF)
@@ -48,11 +67,11 @@
     shape = (KR * group, group * rad_rows)
     row = lax.broadcasted_iota(jnp.int32, shape, 0)
     col = lax.broadcasted_iota(jnp.int32, shape, 1)
-    q = row // group
+    q = part_of(row, group)
     freq = q + jnp.where(q >= KR // 2, total - KR, 0)
-    point = rad * rad_rows + col % rad_rows
-    phase = (freq * point % total).astype(F32) * (2.0 * math.pi / total)
-    same = row % group == col // rad_rows
+    point = rad * rad_rows + rest_of(col, rad_rows)
+    phase = rest_of(freq * point, total).astype(F32) * (2.0 * math.pi / total)
+    same = rest_of(row, group) == part_of(col, rad_rows)
     return jnp.where(same, jnp.cos(phase), 0.0), jnp.where(same, jnp.sin(phase), 0.0)
 
 
@@ -204,7 +223,6 @@
                 r16.at[f, t - 1], rad_in.at[f, t - 1], rs.at[f, t - 1], rr.at[f, t - 1],
                 {"radial": rads[t]},
             )
-            copy.start()
             copies.append(copy)
         return copies
 
@@ -215,21 +233,20 @@
         return jnp.concatenate([value[:, :half], value[:, half:]], axis=0)
 
     rad_g = transform(0)
+    for copy in rad_g:
+        copy.start()
 
     piece = 256
     per = piece // rad_rows
     grads = g_vmem[...].reshape(lines, cols)
+    chooser = chooser_of(lines, channels, rad_rows, F32)
+    match = same_row(rad_rows, lines)
 
     def gram(i, carry):
         block = x_vmem[i // (cut // per), pl.ds(i % (cut // per) * per, per)].reshape(piece, cols)
         full = lax.dot_general(block, grads, (((1,), (1,)), ((), ())), preferred_element_type=F32)
         full = full.reshape(per, rad_rows, lines)
-        row = lax.broadcasted_iota(jnp.int32, full.shape, 1)
-        col = lax.broadcasted_iota(jnp.int32, full.shape, 2) % rad_rows
-        picked = jnp.sum(jnp.where(row == col, full, 0.0), axis=1)
-        line = lax.broadcasted_iota(jnp.int32, (lines, channels), 0) // rad_rows
-        chan = lax.broadcasted_iota(jnp.int32, (lines, channels), 1)
-        chooser = jnp.where(line == chan, 1.0, 0.0).astype(F32)
+        picked = jnp.sum(jnp.where(match[None], full, 0.0), axis=1)
         wl_own[pl.ds(pl.multiple_of(i * per, per), per), :] = jnp.dot(
             picked, chooser, preferred_element_type=F32, precision=lax.Precision.HIGHEST
         )
@@ -257,36 +274,47 @@
     for copy in rad_g:
         copy.wait_recv()
 
-    mode = lax.broadcasted_iota(jnp.int32, (channels, half), 1) % own_k + ax * own_k
+    mode = rest_of(lax.broadcasted_iota(jnp.int32, (channels, half), 1), own_k) + ax * own_k
     scale = jnp.where(mode == 0, 1.0 / points, 2.0 / points)
 
-    def modes(q, carry):
+    lane = rest_of(lax.broadcasted_iota(jnp.int32, (channels, lanes), 1), own_k)
+    pairs = 2 if q_own % 2 == 0 else 1
+
+    def modes(step, carry):
+        sides = [dy_side(step * pairs + j) for j in range(pairs)]
+        for j in range(pairs):
+            mode_back(step * pairs + j, sides[j])
+        return carry
+
+    def dy_side(q):
         g = collect(0, q) * scale
         spec_ref[q, :, half:] = g
         turned = jnp.concatenate([g[:, own_k:], -g[:, :own_k]], axis=1)
         gh, gl = split16(g)
         th, tl = split16(turned)
-        side = jnp.concatenate(
+        return jnp.concatenate(
             [jnp.concatenate([gh, gl], axis=1), jnp.concatenate([th, tl], axis=1)], axis=0
         )
+
+    def mode_back(q, side):
         out = jnp.dot(
             w_vmem[q].reshape(own_k * channels, 2 * channels), side, preferred_element_type=F32
         )
-        lane = lax.broadcasted_iota(jnp.int32, (channels, lanes), 1) % own_k
         total = jnp.zeros((channels, lanes), F32)
         for k in range(own_k):
             total = jnp.where(lane == k, out[k * channels : (k + 1) * channels], total)
         dx = total[:, :half] + total[:, half:]
         dx_all[rad, q] = jnp.concatenate([dx[:cut], dx[cut:]], axis=1).astype(BF)
-        return carry
-
-    lax.fori_loop(0, q_own, modes, 0)
+
+    lax.fori_loop(0, q_own // pairs, modes, 0)
     dx_copies = []
     for t in range(1, n_radial):
         copy = remote(dx_all.at[rad], dx_all.at[rad], ds_.at[t - 1], dr.at[t - 1], {"radial": rads[t]})
         copy.start()
         dx_copies.append(copy)
     sent += dx_copies
+    for copy in rad_x:
+        copy.start()
 
     for copy in wl_copies:
         copy.wait_recv()
@@ -370,7 +398,7 @@
     )
     sh, sl = split16(sides)
     right = jnp.concatenate([sh, sh, sl], axis=0)
-    lane = lax.broadcasted_iota(jnp.int32, (16, 3 * half), 1) % own_k
+    lane = rest_of(lax.broadcasted_iota(jnp.int32, (16, 3 * half), 1), own_k)
     together = 8
     for first in range(0, own_k, together):
         rows = []
@@ -397,22 +425,24 @@
 
     @pl.when(step == 0)
     def _():
-        def products(q, carry):
-            mode_products(KA // n_axial, spec_ref[q], modes_vmem.at[q])
-            store(q).start()
+        pairs = 2 if q_own % 2 == 0 else 1
+
+        def products(i, carry):
+            for j in range(pairs):
+                mode_products(KA // n_axial, spec_ref[i * pairs + j], modes_vmem.at[i * pairs + j])
+            for j in range(pairs):
+                store(i * pairs + j).start()
             return carry
 
-        lax.fori_loop(0, q_own, products, 0)
+        lax.fori_loop(0, q_own // pairs, products, 0)
         wg_out[...] = wg_ref[...]
-        line = lax.broadcasted_iota(jnp.int32, (lines, channels), 0) // rad_rows
-        chan = lax.broadcasted_iota(jnp.int32, (lines, channels), 1)
-        chooser = jnp.where(line == chan, 1.0, 0.0).astype(BF)
+        chooser = chooser_of(lines, channels, rad_rows, BF)
         rows = jnp.dot(chooser, pw_ref[...], preferred_element_type=F32).astype(BF)
         dims = (((1,), (1,)), ((), ()))
         wide = lax.dot_general(rows, chooser, dims, preferred_element_type=F32)
-        row = lax.broadcasted_iota(jnp.int32, wide.shape, 0) % rad_rows
-        col = lax.broadcasted_iota(jnp.int32, wide.shape, 1) % rad_rows
-        left[:, :lines] = jnp.where(row == col, wide, 0.0).astype(BF)
+        match = same_row(rad_rows, lines)
+        wide = jnp.where(match[None], wide.reshape(channels, rad_rows, lines), 0.0)
+        left[:, :lines] = wide.reshape(lines, lines).astype(BF)
         cut = lines // 2
         for d in range(n_axial):
             lanes = slice(lines + d * half, lines + (d + 1) * half)

time: 62 us -> 61 us (0.984)
  Pallas kernels: 60.9 us -> 59.2 us
    pallas_call x1, Pallas kernels: 14 us -> 12.4 us  [body(): pl.pallas_call(functools.partial(final_kernel, n_axial), grid=(steps,), i...]
where the time goes in v3:
time: 61 us; the launch traced here: 60 us
  Pallas kernels  59.2 us (97%)
  between operations  0.8 us (1%)
    pallas_call x1, Pallas kernels, body(): pl.pallas_call(functools.partial(comm_kernel, n_axial, n_radial, 1.0 / ma...  46.8 us
    pallas_call x1, Pallas kernels, body(): pl.pallas_call(functools.partial(final_kernel, n_axial), grid=(steps,), i...  12.4 us

profile of v3, /device:TPU:25, one launch (start us, length us, event | category | flops | bytes accessed | tf_op | source)
XLA Modules:
  0.0 60.0 jit_solution(12808345656624034468)
XLA Ops:
  0.6 46.8 %exchange.1 = (f32[8,64,128]{2,1,0:T(8,128)}, bf16[8,512,128]{2,1,0:T(8,128)(2,1)}, f32[64,64]{1,0:T(8,128)}, bf16[2,32,16,1024]{3,2,1,0:T(8,128)(2,1)}) custom-call(bf16[8,32,64,128]{3,2,1,0:T(8,128)(2,1)} %w_hbm.1, bf16[2,32,16,1024]{3,2,1,0:T(8,128)(2,1)} %bitcast.5, bf16[2,32,16,1024]{3,2,1,0:T(8,128)(2,1)} %bitcast.6, ...), custom_call_target="tpu_custom_call" | custom-call | tf_op jit(solution)/shard_map/exchange/pallas_call | solution.py:495
  47.4 12.4 %input_gradient.1 = (bf16[64,16,1024]{2,1,0:T(8,128)(2,1)}, f32[8,32,64,128]{3,2,1,0:T(8,128)}, f32[64,64]{1,0:T(8,128)}) custom-call(bf16[64,64]{1,0:T(8,128)(2,1)} %pw_ref.1, bf16[64,16,1024]{2,1,0:T(8,128)(2,1)} %bitcast.4, f32[512,128]{1,0:T(8,128)} %constant.16.clone.cl_ref, f32[512,128]{1,0:T(8,128)} %constant.17.clone.sl_ref, ...), custom_call_target="tpu_custom_call" | custom-call | tf_op jit(solution)/shard_map/input_gradient/pallas_call | solution.py:551
